TPU v7x, 512 devices: a whole 4x4x16 slice. The times are simulated.
512 devices in a mesh: seg: 32 (over z_lo, y, core), dev: 16 (over z_hi, x).
Axes of the slice: x: 4, y: 4, z: 16 (z_hi: 4, z_lo: 4; z = z_hi * 4 + z_lo), core: 2. Of those that a mesh axis runs over, the one named last changes fastest.
Arguments:
- queries: bfloat16 [65536, 1536], P(('seg', 'dev')), may hold values from -12 to 12
- keys: bfloat16 [65536, 1536], P(('seg', 'dev')), may hold values from -12 to 12
- values: bfloat16 [65536, 1536], P(('seg', 'dev')), may hold values from -4 to 4
Outputs:
- grad_queries: bfloat16 [65536, 1536], P(('seg', 'dev'))
- grad_keys: bfloat16 [65536, 1536], P(('seg', 'dev'))
- grad_values: bfloat16 [65536, 1536], P(('seg', 'dev'))
All inputs are finite; a program needn't handle non-finite values.
Results may differ from a plain program's by a relative error of at most 0.015.
Values may be sent and summed in bfloat16 or wider, within the bound.
A program may use at most 128 MiB of HBM per device.

v0:
```python
import jax
import jax.numpy as jnp
from jax import lax
from jax.sharding import PartitionSpec as P

HEADS = 16
WINDOW = 256


def passed_along(value, axis, steps):
    count = lax.axis_size(axis)
    initial, last = (max(0, -steps), min(count, count - steps))
    return lax.ppermute(value, axis, [(source, source + steps) for source in range(initial, last)])


def student_pass(block_q, ext_keys, ext_values, target, first_row, head_count):
    row_count, model_width = block_q.shape
    ext_count = ext_keys.shape[0]
    reach_rows = ext_count - row_count
    head_dim = model_width // head_count
    factor = head_dim ** (-0.5)
    query_heads = block_q.reshape(row_count, head_count, head_dim)
    key_heads = ext_keys.reshape(ext_count, head_count, head_dim)
    value_heads = ext_values.reshape(ext_count, head_count, head_dim)
    scores = (
        jnp.einsum("fhd,ehd->hfe", query_heads, key_heads, preferred_element_type=jnp.float32)
        * factor
    )
    query_pos = first_row + lax.iota(jnp.int32, row_count)
    key_pos = first_row - reach_rows + lax.iota(jnp.int32, ext_count)
    allowed = (
        (key_pos[None, :] <= query_pos[:, None])
        & (key_pos[None, :] >= query_pos[:, None] - reach_rows)
        & (key_pos[None, :] >= 0)
    )
    scores = jnp.where(allowed[None], scores, -1e30)
    row_max = scores.max(-1, keepdims=True)
    numerators = jnp.exp(scores - row_max)
    probability = numerators / numerators.sum(-1, keepdims=True)
    weights = probability.astype(jnp.bfloat16)
    output = jnp.einsum(
        "hfe,ehd->fhd", weights, value_heads, preferred_element_type=jnp.float32
    ).reshape(row_count, model_width)
    d_out = (128.0 * (output - target.astype(jnp.float32))).astype(jnp.bfloat16)
    d_out = d_out.reshape(row_count, head_count, head_dim)
    grad_v = jnp.einsum("hfe,fhd->ehd", weights, d_out, preferred_element_type=jnp.float32)
    d_prob = jnp.einsum("fhd,ehd->hfe", d_out, value_heads, preferred_element_type=jnp.float32)
    row_inner = (probability * d_prob).sum(-1, keepdims=True)
    d_scores = (probability * (d_prob - row_inner) * factor).astype(jnp.bfloat16)
    grad_q = jnp.einsum("hfe,ehd->fhd", d_scores, key_heads, preferred_element_type=jnp.float32)
    grad_k = jnp.einsum("hfe,fhd->ehd", d_scores, query_heads, preferred_element_type=jnp.float32)
    return (
        grad_q.reshape(row_count, model_width),
        grad_k.reshape(ext_count, model_width),
        grad_v.reshape(ext_count, model_width),
    )


def local(queries, keys, values):
    row_count, model_width = queries.shape
    head_count = HEADS
    head_dim = model_width // head_count
    factor = head_dim ** (-0.5)
    query_heads = queries.reshape(row_count, head_count, head_dim)
    start_state = (
        jnp.full((head_count, row_count), -1e30, jnp.float32),
        jnp.zeros((head_count, row_count), jnp.float32),
        jnp.zeros((row_count, head_count, head_dim), jnp.float32),
    )
    absorb_key_piece = lax.all_gather(keys, "dev", axis=0, tiled=True)
    absorb_value_piece = lax.all_gather(values, "dev", axis=0, tiled=True)
    piece_rows = absorb_key_piece.shape[0]
    block_rows = 256
    key_blocks = absorb_key_piece.reshape(
        piece_rows // block_rows, block_rows, head_count, head_dim
    )
    value_blocks = absorb_value_piece.reshape(
        piece_rows // block_rows, block_rows, head_count, head_dim
    )

    def one_block(block_index, inner_state):
        run_max, run_total, run_acc = inner_state
        key_block = key_blocks[block_index]
        value_block = value_blocks[block_index]
        scores = (
            jnp.einsum("fhd,khd->hfk", query_heads, key_block, preferred_element_type=jnp.float32)
            * factor
        )
        new_max = jnp.maximum(run_max, scores.max(-1))
        old_scale = jnp.exp(run_max - new_max)
        numerators = jnp.exp(scores - new_max[..., None])
        new_total = run_total * old_scale + numerators.sum(-1)
        addend = jnp.einsum(
            "hfk,khd->fhd",
            numerators.astype(jnp.bfloat16),
            value_block,
            preferred_element_type=jnp.float32,
        )
        new_acc = run_acc * jnp.transpose(old_scale)[:, :, None] + addend
        return (new_max, new_total, new_acc)

    run_max, run_total, run_acc = lax.fori_loop(0, piece_rows // block_rows, one_block, start_state)
    target = (
        (run_acc / jnp.transpose(run_total)[:, :, None])
        .reshape(row_count, model_width)
        .astype(jnp.bfloat16)
    )
    reach_count = -(-WINDOW // row_count)
    halo_keys = []
    halo_values = []
    for back_step in range(reach_count, 0, -1):
        key_piece, value_piece = passed_along((keys, values), ("seg", "dev"), back_step)
        halo_keys.append(key_piece)
        halo_values.append(value_piece)
    ext_keys = jnp.concatenate([jnp.concatenate(halo_keys, 0), keys], 0)
    ext_values = jnp.concatenate([jnp.concatenate(halo_values, 0), values], 0)
    first_row = lax.axis_index(("seg", "dev")) * row_count
    grad_q, grad_k, grad_v = student_pass(
        queries, ext_keys, ext_values, target, first_row, head_count
    )
    pad_rows = reach_count * row_count - WINDOW
    zero_rows = jnp.zeros((pad_rows, model_width), jnp.bfloat16)
    halo_grad_k = jnp.concatenate([zero_rows, grad_k[:WINDOW].astype(jnp.bfloat16)], 0)
    halo_grad_v = jnp.concatenate([zero_rows, grad_v[:WINDOW].astype(jnp.bfloat16)], 0)
    local_k = grad_k[WINDOW:]
    local_v = grad_v[WINDOW:]
    for back_step in range(reach_count, 0, -1):
        offset_rows = (reach_count - back_step) * row_count
        piece_k = halo_grad_k[offset_rows : offset_rows + row_count]
        piece_v = halo_grad_v[offset_rows : offset_rows + row_count]
        back_k, back_v = passed_along((piece_k, piece_v), ("seg", "dev"), -back_step)
        local_k = local_k + back_k.astype(jnp.float32)
        local_v = local_v + back_v.astype(jnp.float32)
    return (grad_q.astype(jnp.bfloat16), local_k.astype(jnp.bfloat16), local_v.astype(jnp.bfloat16))


def solution(mesh):
    in_specs = (P(("seg", "dev"), None), P(("seg", "dev"), None), P(("seg", "dev"), None))
    out_specs = (P(("seg", "dev"), None), P(("seg", "dev"), None), P(("seg", "dev"), None))
    return jax.shard_map(local, mesh=mesh, in_specs=in_specs, out_specs=out_specs, check_vma=False)
```

profile of v0, /device:TPU:36, one launch (start us, length us, event | category | flops | bytes accessed | tf_op | source)
XLA Modules:
  0.0 665.9 jit_solution(2360740809766414248)
XLA Ops:
  7.2 0.7 all-gather.3.cloned.1.call-update
  7.9 0.7 all-gather.5.cloned.1.call-update
  8.6 3.1 collective-permute-start.1
  11.8 9.3 %collective-permute-start = (bf16[128,1536]{1,0:T(8,128)(2,1)}, bf16[128,1536]{1,0:T(8,128)(2,1)}, u32[]{:S(2)}, u32[]{:S(2)}) collective-permute-start(bf16[128,1536]{1,0:T(8,128)(2,1)} %param.6), channel_id=1, source_target_pairs={{0,2},{1,3},{2,4},{3,5},{4,6},{5,7},{6,8},{7,9},{8,10},{9,11},{10,... | collective-permute-start | bytes 1179656 | tf_op jit(solution)/shard_map/ppermute | solution.py:13
  21.1 4.0 collective-permute-start.3
  25.1 8.1 %collective-permute-start.2 = (bf16[128,1536]{1,0:T(8,128)(2,1)}, bf16[128,1536]{1,0:T(8,128)(2,1)}, u32[]{:S(2)}, u32[]{:S(2)}) collective-permute-start(bf16[128,1536]{1,0:T(8,128)(2,1)} %param.7), channel_id=1, source_target_pairs={{0,2},{1,3},{2,4},{3,5},{4,6},{5,7},{6,8},{7,9},{8,10},{9,11},{10,... | collective-permute-start | bytes 1179656 | tf_op jit(solution)/shard_map/ppermute | solution.py:13
  33.3 1.3 copy.25
  34.8 0.7 copy-done.3
  35.6 43.7 %collective-permute-done = bf16[128,1536]{1,0:T(8,128)(2,1)} collective-permute-done((bf16[128,1536]{1,0:T(8,128)(2,1)}, bf16[128,1536]{1,0:T(8,128)(2,1)}, u32[]{:S(2)}, u32[]{:S(2)}) %collective-permute-start) | collective-permute-done | bytes 393248 | tf_op jit(solution)/shard_map/ppermute | solution.py:13
  79.3 1.3 pad_maximum_fusion
  80.6 1.5 copy.24
  82.1 11.5 %collective-permute-done.2 = bf16[128,1536]{1,0:T(8,128)(2,1)} collective-permute-done((bf16[128,1536]{1,0:T(8,128)(2,1)}, bf16[128,1536]{1,0:T(8,128)(2,1)}, u32[]{:S(2)}, u32[]{:S(2)}) %collective-permute-start.2) | collective-permute-done | bytes 393248 | tf_op jit(solution)/shard_map/ppermute | solution.py:13
  93.6 1.1 pad_maximum_fusion.1
  94.7 1.5 copy.26
  96.1 4.2 fusion.55
  100.3 183.1 %all-gather.3.cloned.1.call-done = bf16[2048,1536]{1,0:T(8,128)(2,1)} async-done(((bf16[128,1536]{1,0:T(8,128)(2,1)}), bf16[2048,1536]{1,0:T(8,128)(2,1)}) %all-gather.3.cloned.1.call-update) | async-done | bytes 6291472 | tf_op jit(solution)/shard_map/all_gather | solution.py:70
  283.4 13.7 %reshape.136 = bf16[8,256,16,96]{3,2,1,0:T(8,128)(2,1)} reshape(bf16[2048,1536]{1,0:T(8,128)(2,1)} %all-gather.3.cloned.1.call-done) | data formatting | bytes 12582912 | tf_op jit(solution)/shard_map/reshape | solution.py:74
  297.1 11.8 %copy.30 = bf16[8,256,16,96]{1,3,2,0:T(8,128)(2,1)} copy(bf16[8,256,16,96]{3,2,1,0:T(8,128)(2,1)} %reshape.136) | data formatting | bytes 12582912
  308.8 111.1 %all-gather.5.cloned.1.call-done = bf16[2048,1536]{1,0:T(8,128)(2,1)} async-done(((bf16[128,1536]{1,0:T(8,128)(2,1)}), bf16[2048,1536]{1,0:T(8,128)(2,1)}) %all-gather.5.cloned.1.call-update) | async-done | bytes 6291472 | tf_op jit(solution)/shard_map/all_gather | solution.py:71
  419.9 13.7 %reshape.137 = bf16[8,256,16,96]{3,2,1,0:T(8,128)(2,1)} reshape(bf16[2048,1536]{1,0:T(8,128)(2,1)} %all-gather.5.cloned.1.call-done) | data formatting | bytes 12582912 | tf_op jit(solution)/shard_map/reshape | solution.py:77
  433.6 11.7 %copy.31 = bf16[8,256,16,96]{1,3,2,0:T(8,128)(2,1)} copy(bf16[8,256,16,96]{3,2,1,0:T(8,128)(2,1)} %reshape.137) | data formatting | bytes 12582912
  445.2 31.1 %while.18 = (s32[]{:T(128)}, f32[16,128]{1,0:T(8,128)S(1)}, f32[16,128]{1,0:T(8,128)S(1)}, f32[128,16,96]{0,2,1:T(8,128)S(1)}, bf16[8,256,16,96]{1,3,2,0:T(8,128...) while((s32[]{:T(128)}, f32[16,128]{1,0:T(8,128)S(1)}, ...), condition=%wide.region_5.6_spmd.clone, body=%wide.region_2.5_spmd.clone.sunk | while | flops 206123008 | bytes 9961593 | solution.py:102
  445.2 1.6 bitcast_reduce_fusion.2
  446.9 0.4 fusion.83
  447.3 1.8 fusion.85
  449.1 1.6 bitcast_reduce_fusion.2
  450.8 0.4 fusion.83
  451.2 1.8 fusion.85
  453.0 1.6 bitcast_reduce_fusion.2
  455.1 1.8 fusion.85
  456.9 1.6 bitcast_reduce_fusion.2
  458.6 0.4 fusion.83
  459.0 1.8 fusion.85
  460.8 1.6 bitcast_reduce_fusion.2
  462.4 0.4 fusion.83
  462.9 1.8 fusion.85
  464.7 1.6 bitcast_reduce_fusion.2
  466.3 0.4 fusion.83
  466.7 1.8 fusion.85
  468.6 1.6 bitcast_reduce_fusion.2
  470.2 0.4 fusion.83
  470.6 1.8 fusion.85
  472.5 1.6 bitcast_reduce_fusion.2
  474.1 0.4 fusion.83
  474.5 1.8 fusion.85
  476.4 2.8 fusion.39
  479.2 2.3 fusion.60
  481.8 2.8 fusion.59
  484.6 7.6 %fusion.56 = (bf16[384,16,96]{0,2,1:T(8,128)(2,1)}, f32[384,16,96]{0,2,1:T(8,128)}) fusion(bf16[128,16,96]{0,2,1:T(8,128)(2,1)S(1)} %get-tuple-element.277, f32[16,128,384]{1,2,0:T(8,128)} %fusion.60, f32[16,128,384]{1,2,0:T(8,128)} %get-tuple-element.190, f32[16,128]{1,0:T(8,128)S(1)} %get-tuple-element.189), kind=kOutput, calls=%fused_computation.68 | convolution fusion | flops 157092224 | bytes 10231808 | tf_op jit(solution)/shard_map/hfe,fhd->ehd/dot_general | solution.py:51
  492.3 1.3 fusion.54
  493.7 2.5 collective-permute-start.5
  496.4 52.0 %collective-permute-start.4 = (bf16[128,1536]{1,0:T(8,128)(2,1)S(1)}, bf16[128,1536]{1,0:T(8,128)(2,1)}, u32[]{:S(2)}, u32[]{:S(2)}) collective-permute-start(bf16[128,1536]{1,0:T(8,128)(2,1)S(1)} %copy.36), channel_id=1, source_target_pairs={{2,0},{3,1},{4,2},{5,3},{6,4},{7,5},{8,6},{9,7},{10,8},{11,9},{12,... | collective-permute-start | bytes 1179656 | tf_op jit(solution)/shard_map/ppermute | solution.py:13
  548.3 5.9 fusion.40
  554.2 0.9 copy.43
  555.2 1.2 slice.58
  556.6 1.2 fusion.53
  557.8 0.9 copy.42
  558.7 1.9 collective-permute-start.7
  560.6 1.2 slice.61
  562.3 3.4 collective-permute-start.6
  565.7 2.0 add_convert_fusion.1
  567.7 1.0 collective-permute-done.7
  568.7 88.5 %collective-permute-done.6 = bf16[128,1536]{1,0:T(8,128)(2,1)S(1)} collective-permute-done((bf16[128,1536]{1,0:T(8,128)(2,1)S(1)}, bf16[128,1536]{1,0:T(8,128)(2,1)S(1)}, u32[]{:S(2)}, u32[]{:S(2)}) %collective-permute-start.6) | collective-permute-done | bytes 393248 | tf_op jit(solution)/shard_map/ppermute | solution.py:13
  657.2 1.9 add_convert_fusion
  (52 shorter events, 2.3 us)
Async XLA Ops:
  7.2 276.2 %all-gather.3.cloned.1.call-start = ((), (), s32[]{:S(2)}) async-start(), calls=%async_computation | async-start | bytes 6684672 | tf_op jit(solution)/shard_map/all_gather | solution.py:70
  7.9 412.0 %all-gather.5.cloned.1.call-start = ((), (), s32[]{:S(2)}) async-start(), calls=%async_computation.1 | async-start | bytes 6684672 | tf_op jit(solution)/shard_map/all_gather | solution.py:71
  8.6 26.2 %collective-permute-start.1 = (bf16[128,1536]{1,0:T(8,128)(2,1)}, bf16[128,1536]{1,0:T(8,128)(2,1)S(1)}, u32[]{:S(2)}, u32[]{:S(2)}) collective-permute-start(bf16[128,1536]{1,0:T(8,128)(2,1)} %param.6), channel_id=1, source_target_pairs={{0,1},{1,2},{2,3},{3,4},{4,5},{5,6},{6,7},{7,8},{8,9},{9,10},{10,1... | collective-permute-start | bytes 1179656 | tf_op jit(solution)/shard_map/ppermute | solution.py:13
  11.8 67.6 %collective-permute-start = (bf16[128,1536]{1,0:T(8,128)(2,1)}, bf16[128,1536]{1,0:T(8,128)(2,1)}, u32[]{:S(2)}, u32[]{:S(2)}) collective-permute-start(bf16[128,1536]{1,0:T(8,128)(2,1)} %param.6), channel_id=1, source_target_pairs={{0,2},{1,3},{2,4},{3,5},{4,6},{5,7},{6,8},{7,9},{8,10},{9,11},{10,... | collective-permute-start | bytes 1179656 | tf_op jit(solution)/shard_map/ppermute | solution.py:13
  21.1 61.0 %collective-permute-start.3 = (bf16[128,1536]{1,0:T(8,128)(2,1)}, bf16[128,1536]{1,0:T(8,128)(2,1)S(1)}, u32[]{:S(2)}, u32[]{:S(2)}) collective-permute-start(bf16[128,1536]{1,0:T(8,128)(2,1)} %param.7), channel_id=1, source_target_pairs={{0,1},{1,2},{2,3},{3,4},{4,5},{5,6},{6,7},{7,8},{8,9},{9,10},{10,1... | collective-permute-start | bytes 1179656 | tf_op jit(solution)/shard_map/ppermute | solution.py:13
  25.1 68.5 %collective-permute-start.2 = (bf16[128,1536]{1,0:T(8,128)(2,1)}, bf16[128,1536]{1,0:T(8,128)(2,1)}, u32[]{:S(2)}, u32[]{:S(2)}) collective-permute-start(bf16[128,1536]{1,0:T(8,128)(2,1)} %param.7), channel_id=1, source_target_pairs={{0,2},{1,3},{2,4},{3,5},{4,6},{5,7},{6,8},{7,9},{8,10},{9,11},{10,... | collective-permute-start | bytes 1179656 | tf_op jit(solution)/shard_map/ppermute | solution.py:13
  34.8 58.8 %copy-start.1 = (bf16[128,1536]{1,0:T(8,128)(2,1)S(1)}, bf16[128,1536]{1,0:T(8,128)(2,1)}, u32[]{:S(2)}) copy-start(bf16[128,1536]{1,0:T(8,128)(2,1)} %param.7) | copy-start | bytes 1179652
  34.8 0.7 copy-start.3
  476.4 2.9 copy-start
  479.2 2.6 copy-start.4
  492.3 56.1 %copy-start.2 = (bf16[384,1536]{0,1:T(8,128)(2,1)S(1)}, bf16[384,1536]{0,1:T(8,128)(2,1)}, u32[]{:S(2)}) copy-start(bf16[384,1536]{0,1:T(8,128)(2,1)} %copy.24) | copy-start | bytes 3538948
  493.7 72.0 %collective-permute-start.5 = (bf16[128,1536]{1,0:T(8,128)(2,1)S(1)}, bf16[128,1536]{1,0:T(8,128)(2,1)}, u32[]{:S(2)}, u32[]{:S(2)}) collective-permute-start(bf16[128,1536]{1,0:T(8,128)(2,1)S(1)} %copy.38), channel_id=1, source_target_pairs={{1,0},{2,1},{3,2},{4,3},{5,4},{6,5},{7,6},{8,7},{9,8},{10,9},{11,1... | collective-permute-start | bytes 1179656 | tf_op jit(solution)/shard_map/ppermute | solution.py:13
  496.4 69.3 %collective-permute-start.4 = (bf16[128,1536]{1,0:T(8,128)(2,1)S(1)}, bf16[128,1536]{1,0:T(8,128)(2,1)}, u32[]{:S(2)}, u32[]{:S(2)}) collective-permute-start(bf16[128,1536]{1,0:T(8,128)(2,1)S(1)} %copy.36), channel_id=1, source_target_pairs={{2,0},{3,1},{4,2},{5,3},{6,4},{7,5},{8,6},{9,7},{10,8},{11,9},{12,... | collective-permute-start | bytes 1179656 | tf_op jit(solution)/shard_map/ppermute | solution.py:13
  558.7 10.0 %collective-permute-start.7 = (bf16[128,1536]{1,0:T(8,128)(2,1)}, bf16[128,1536]{1,0:T(8,128)(2,1)}, u32[]{:S(2)}, u32[]{:S(2)}) collective-permute-start(bf16[128,1536]{1,0:T(8,128)(2,1)} %copy.42), channel_id=1, source_target_pairs={{1,0},{2,1},{3,2},{4,3},{5,4},{6,5},{7,6},{8,7},{9,8},{10,9},{11,1... | collective-permute-start | bytes 1179656 | tf_op jit(solution)/shard_map/ppermute | solution.py:13
  562.3 94.9 %collective-permute-start.6 = (bf16[128,1536]{1,0:T(8,128)(2,1)S(1)}, bf16[128,1536]{1,0:T(8,128)(2,1)S(1)}, u32[]{:S(2)}, u32[]{:S(2)}) collective-permute-start(bf16[128,1536]{1,0:T(8,128)(2,1)S(1)} %copy.40), channel_id=1, source_target_pairs={{2,0},{3,1},{4,2},{5,3},{6,4},{7,5},{8,6},{9,7},{10,8},{11,9},{12,... | collective-permute-start | bytes 1179656 | tf_op jit(solution)/shard_map/ppermute | solution.py:13
Sparse Core Ops, SparseCore 0:
  11.0 272.3 all-gather.2
  286.4 133.4 all-gather.4
where the time goes:
time: 668 us; the launch traced here: 666 us
  waiting for transfers between devices  440 us (66%)
  starting transfers between devices  84.4 us (13%)
  local copies, waits for them, and re-layouts  63.8 us (10%)
  matrix products  53.1 us (8%)
  between operations  14.3 us (2%)
  other arithmetic  9.59 us (1%)
    all_gather x1, waiting for transfers between devices, local(): absorb_key_piece = lax.all_gather(keys, 'dev', axis=0, tiled=True)  183 us
    ppermute x8, waiting for transfers between devices, passed_along(): lax.ppermute(value, axis, [(source, source + steps) for source in range(i...  145 us
    all_gather x1, waiting for transfers between devices, local(): absorb_value_piece = lax.all_gather(values, 'dev', axis=0, tiled=True)  111 us
    ppermute x8, starting transfers between devices, passed_along(): lax.ppermute(value, axis, [(source, source + steps) for source in range(i...  84.3 us
    unnamed x14, local copies, waits for them, and re-layouts  26.7 us
    dot_general x8, matrix products, one_block(): jnp.einsum('hfk,khd->fhd', numerators.astype(jnp.bfloat16), value_block,...  14.5 us
    reshape x1, local copies, waits for them, and re-layouts, local(): absorb_key_piece.reshape(piece_rows // block_rows, block_rows, head_count...  13.7 us
    reshape x1, local copies, waits for them, and re-layouts, local(): absorb_value_piece.reshape(piece_rows // block_rows, block_rows, head_cou...  13.7 us
  transfers between devices with their start and end apart: 10, of which 6 were waited for; matrix products, arithmetic and copies ran while one was open for 8% of the time, Pallas kernels for 0%

commit v1 on v0

v1 whole, which is shorter than its diff:
```python
import functools

import jax
import jax.numpy as jnp
from jax import lax
from jax.experimental import pallas as pl
from jax.experimental.pallas import tpu as pltpu
from jax.sharding import PartitionSpec as P

HEADS = 16
WINDOW = 256
MESH = pl.DeviceIdType.MESH
F32 = jnp.float32
BF16 = jnp.bfloat16
LOG2E = 1.4426950408889634
CONTRACT_LANES = (((1,), (1,)), ((), ()))


def transposed(tile):
    return tile.astype(F32).T.astype(BF16)


def kernel(
    n_dev,
    n_seg,
    q_ref,
    k_ref,
    v_ref,
    gq_ref,
    gk_ref,
    gv_ref,
    send,
    recv,
    halo,
    feat,
    rows,
    acc,
    far_out,
    far_in,
    out_send,
    out_recv,
    in_ssem,
    in_rsem,
    halo_ssem,
    halo_rsem,
    far_ssem,
    far_rsem,
    out_ssem,
    out_rsem,
):
    me = lax.axis_index("dev")
    seg = lax.axis_index("seg")
    frames, width = q_ref.shape
    dim = width // n_dev
    far_blocks = WINDOW // frames
    segment = n_dev * frames
    ext = WINDOW + frames
    factor = dim ** (-0.5)
    next_seg = lax.rem(seg + 1, n_seg)
    prev_seg = lax.rem(seg + n_seg - 1, n_seg)
    tiles = width // 128

    def head_rows(d):
        return pl.ds(pl.multiple_of(d * dim, 32), dim)

    def frame_cols(block, count):
        return pl.ds(pl.multiple_of(block * frames, 128), count)

    barrier = pltpu.get_barrier_semaphore()
    for i in range(1, n_dev):
        pl.semaphore_signal(
            barrier, inc=1, device_id={"dev": lax.rem(me + i, n_dev)}, device_id_type=MESH
        )
    pl.semaphore_signal(barrier, inc=1, device_id={"seg": next_seg}, device_id_type=MESH)
    pl.semaphore_signal(barrier, inc=1, device_id={"seg": prev_seg}, device_id_type=MESH)

    def to_features(ref, a):
        for t in range(tiles):
            send[a, t * 128 : (t + 1) * 128, :] = transposed(ref[:, t * 128 : (t + 1) * 128])
        recv[a, me] = send[a, head_rows(me), :]

    def in_copy(a, d, slot, sem_at):
        return pltpu.make_async_remote_copy(
            src_ref=send.at[a, head_rows(d)],
            dst_ref=recv.at[a, slot],
            send_sem=in_ssem.at[a, d],
            recv_sem=in_rsem.at[a, sem_at],
            device_id={"dev": d},
            device_id_type=MESH,
        )

    def send_in(a):
        def body(i, carry):
            d = lax.rem(me + i, n_dev)
            in_copy(a, d, me, me).start()
            return carry

        lax.fori_loop(1, n_dev, body, 0)

    to_features(k_ref, 1)
    to_features(v_ref, 2)
    pl.semaphore_wait(barrier, n_dev + 1)
    send_in(1)
    send_in(2)
    to_features(q_ref, 0)
    send_in(0)

    acc[...] = jnp.zeros_like(acc)

    def place(a, block, piece):
        feat[a - 1, :, frame_cols(block, frames)] = piece
        rows[a - 1, frame_cols(block, frames), :] = transposed(piece)

    def gather(i, carry):
        src = lax.rem(me - i + n_dev, n_dev)
        for a in (1, 2):

            @pl.when(i > 0)
            def _():
                in_copy(a, src, src, src).wait_recv()

            place(a, src + far_blocks, recv[a, src])
        return carry

    lax.fori_loop(0, n_dev, gather, 0)

    def halo_copy(a):
        return pltpu.make_async_remote_copy(
            src_ref=recv.at[a, pl.ds(n_dev - far_blocks, far_blocks)],
            dst_ref=halo.at[a - 1],
            send_sem=halo_ssem.at[a - 1],
            recv_sem=halo_rsem.at[a - 1],
            device_id={"seg": next_seg},
            device_id_type=MESH,
        )

    for a in (1, 2):
        halo_copy(a).start()
    for a in (1, 2):
        halo_copy(a).wait_recv()
        for b in range(far_blocks):
            place(a, b, halo[a - 1, b])

    def out_copy(a, d, sem_at, head):
        return pltpu.make_async_remote_copy(
            src_ref=out_send.at[a, d],
            dst_ref=out_recv.at[a, head_rows(head)],
            send_sem=out_ssem.at[a, d],
            recv_sem=out_rsem.at[a, sem_at],
            device_id={"dev": d},
            device_id_type=MESH,
        )

    def give(a, block, value):
        @pl.when(block == me)
        def _():
            out_recv[a, head_rows(me), :] = value

        @pl.when(block != me)
        def _():
            out_send[a, block] = value
            out_copy(a, block, me, me).start()

    def give_keys(block):
        for a in (1, 2):
            give(a, block, acc[a - 1, block + far_blocks].astype(BF16))

    def far_copy():
        return pltpu.make_async_remote_copy(
            src_ref=far_out,
            dst_ref=far_in,
            send_sem=far_ssem,
            recv_sem=far_rsem,
            device_id={"seg": prev_seg},
            device_id_type=MESH,
        )

    key_at = lax.broadcasted_iota(jnp.int32, (ext, frames), 0)
    query_at = lax.broadcasted_iota(jnp.int32, (ext, frames), 1)
    in_window = (key_at >= query_at) & (key_at <= query_at + WINDOW)

    def one_block(s, carry):
        block = lax.rem(me - s + n_dev, n_dev)

        @pl.when(s > 0)
        def _():
            in_copy(0, block, block, block).wait_recv()

        q_feat = recv[0, block]
        scores = jnp.dot(
            rows[0, WINDOW : WINDOW + segment, :], q_feat, preferred_element_type=F32
        ) * (factor * LOG2E)
        numer = jnp.exp2(scores - scores.max(0, keepdims=True))
        total = numer.sum(0, keepdims=True)
        summed = jnp.dot(
            feat[1, :, WINDOW : WINDOW + segment], numer.astype(BF16), preferred_element_type=F32
        )
        target = (summed / total).astype(BF16).astype(F32)

        span = frame_cols(block, ext)
        first = (seg * n_dev + block) * frames - WINDOW
        allowed = in_window & (key_at + first >= 0)
        near = jnp.dot(rows[0, span, :], q_feat, preferred_element_type=F32) * (factor * LOG2E)
        near = jnp.where(allowed, near, -1e30)
        near_numer = jnp.exp2(near - near.max(0, keepdims=True))
        prob = near_numer / near_numer.sum(0, keepdims=True)
        weights = prob.astype(BF16)
        student = jnp.dot(feat[1, :, span], weights, preferred_element_type=F32)
        d_out = (128.0 * (student - target)).astype(BF16)
        d_prob = jnp.dot(rows[1, span, :], d_out, preferred_element_type=F32)
        inner = (prob * d_prob).sum(0, keepdims=True)
        d_scores = (prob * (d_prob - inner) * factor).astype(BF16)
        grad_q = jnp.dot(feat[0, :, span], d_scores, preferred_element_type=F32)
        grad_k = lax.dot_general(q_feat, d_scores, CONTRACT_LANES, preferred_element_type=F32)
        grad_v = lax.dot_general(d_out, weights, CONTRACT_LANES, preferred_element_type=F32)
        for b in range(far_blocks + 1):
            cols = slice(b * frames, (b + 1) * frames)
            acc[0, block + b] += grad_k[:, cols]
            acc[1, block + b] += grad_v[:, cols]
        give(0, block, grad_q.astype(BF16))

        last_first = jnp.where(me >= far_blocks - 1, 0, me + 1)

        @pl.when(block == last_first)
        def _():
            far_out[...] = acc[:, 0:far_blocks].astype(BF16)
            far_copy().start()

        @pl.when((s >= far_blocks) & (block < n_dev - far_blocks))
        def _():
            give_keys(block)

        return carry

    lax.fori_loop(0, n_dev, one_block, 0)

    for s in range(far_blocks):
        block = lax.rem(me - s + n_dev, n_dev)

        @pl.when(block < n_dev - far_blocks)
        def _():
            give_keys(block)

    far_copy().wait_recv()
    for b in range(far_blocks):
        for a in range(2):
            acc[a, n_dev + b] += far_in[a, b].astype(F32)
        give_keys(n_dev - far_blocks + b)

    group = 384 // dim
    for a, out in ((0, gq_ref), (1, gk_ref), (2, gv_ref)):
        for g in range(n_dev // group):
            for i in range(group):
                head = g * group + i

                @pl.when(head != me)
                def _():
                    out_copy(a, head, head, head).wait_recv()

            for t in range(3 * g, 3 * g + 3):
                cols = slice(t * 128, (t + 1) * 128)
                out[:, cols] = transposed(out_recv[a, cols, :])

    def drain(i, carry):
        d = lax.rem(me + i, n_dev)
        for a in range(3):
            in_copy(a, d, me, me).wait_send()
            out_copy(a, d, me, me).wait_send()
        return carry

    lax.fori_loop(1, n_dev, drain, 0)
    for a in (1, 2):
        halo_copy(a).wait_send()
    far_copy().wait_send()


def local(n_dev, n_seg, queries, keys, values):
    frames, width = queries.shape
    dim = width // n_dev
    far_blocks = WINDOW // frames
    held = n_dev + far_blocks
    vmem = pl.BlockSpec(memory_space=pltpu.VMEM)
    dma = pltpu.SemaphoreType.DMA
    return pl.pallas_call(
        functools.partial(kernel, n_dev, n_seg),
        out_shape=[jax.ShapeDtypeStruct((frames, width), BF16)] * 3,
        in_specs=[vmem] * 3,
        out_specs=[vmem] * 3,
        scratch_shapes=[
            pltpu.VMEM((3, width, frames), BF16),
            pltpu.VMEM((3, n_dev, dim, frames), BF16),
            pltpu.VMEM((2, far_blocks, dim, frames), BF16),
            pltpu.VMEM((2, dim, held * frames), BF16),
            pltpu.VMEM((2, held * frames, dim), BF16),
            pltpu.VMEM((2, held, dim, frames), F32),
            pltpu.VMEM((2, far_blocks, dim, frames), BF16),
            pltpu.VMEM((2, far_blocks, dim, frames), BF16),
            pltpu.VMEM((3, n_dev, dim, frames), BF16),
            pltpu.VMEM((3, width, frames), BF16),
            dma((3, n_dev)),
            dma((3, n_dev)),
            dma((2,)),
            dma((2,)),
            dma,
            dma,
            dma((3, n_dev)),
            dma((3, n_dev)),
        ],
        compiler_params=pltpu.CompilerParams(
            collective_id=0, has_side_effects=True, vmem_limit_bytes=48 << 20
        ),
        name="heads_exchange",
    )(queries, keys, values)


def solution(mesh):
    n_dev, n_seg = mesh.shape["dev"], mesh.shape["seg"]
    rows = P(("seg", "dev"), None)
    return jax.shard_map(
        functools.partial(local, n_dev, n_seg),
        mesh=mesh,
        in_specs=(rows, rows, rows),
        out_specs=(rows, rows, rows),
        check_vma=False,
    )
```

time: 668 us -> 138 us (0.21)
  the two profiles are of different devices: /device:TPU:36 before, /device:TPU:57 now
where the time goes in v1:
time: 138 us
  Pallas kernels  132 us (96%)
  local copies, waits for them, and re-layouts  5.22 us (4%)
    pallas_call x1, Pallas kernels, local(): pl.pallas_call(functools.partial(kernel, n_dev, n_seg), out_shape=[jax.Sh...  132 us
    unnamed x9, local copies, waits for them, and re-layouts  5.22 us

profile of v1, /device:TPU:57, one launch (start us, length us, event | category | flops | bytes accessed | tf_op | source)
XLA Modules:
  0.0 137.6 jit_solution(1629895914456075471)
XLA Ops:
  0.6 0.0 copy-start
  0.6 1.0 copy-done
  1.6 0.0 copy-start.1
  1.6 1.0 copy-done.1
  2.6 0.0 copy-start.2
  2.6 1.0 copy-done.2
  3.6 131.7 %heads_exchange.1 = (bf16[128,1536]{1,0:T(8,128)(2,1)S(1)}, bf16[128,1536]{1,0:T(8,128)(2,1)S(1)}, bf16[128,1536]{1,0:T(8,128)(2,1)S(1)}) custom-call(bf16[128,1536]{1,0:T(8,128)(2,1)S(1)} %copy-done, bf16[128,1536]{1,0:T(8,128)(2,1)S(1)} %copy-done.1, bf16[128,1536]{1,0:T(8,128)(2,1)S(1)} %copy-done.2), custom_call_target="tpu_custom_call" | custom-call | tf_op jit(solution)/shard_map/heads_exchange/pallas_call | solution.py:284
  135.3 0.7 copy.9
  136.1 0.7 copy.10
  136.8 0.7 copy.11
Async XLA Ops:
  0.6 1.0 copy-start
  1.6 1.0 copy-start.1
  2.6 1.0 copy-start.2

commit v2 on v1

--- a/solution.py
+++ b/solution.py
@@ -17,7 +17,7 @@
 
 
 def transposed(tile):
-    return tile.astype(F32).T.astype(BF16)
+    return tile.T
 
 
 def kernel(
@@ -29,6 +29,7 @@
     gq_ref,
     gk_ref,
     gv_ref,
+    held_in,
     send,
     recv,
     halo,
@@ -47,10 +48,17 @@
     far_rsem,
     out_ssem,
     out_rsem,
+    load_sem,
 ):
     me = lax.axis_index("dev")
     seg = lax.axis_index("seg")
     frames, width = q_ref.shape
+    loads = [
+        pltpu.make_async_copy(ref, held_in.at[a], load_sem.at[a])
+        for a, ref in ((0, q_ref), (1, k_ref), (2, v_ref))
+    ]
+    for a in (1, 2, 0):
+        loads[a].start()
     dim = width // n_dev
     far_blocks = WINDOW // frames
     segment = n_dev * frames
@@ -74,9 +82,11 @@
     pl.semaphore_signal(barrier, inc=1, device_id={"seg": next_seg}, device_id_type=MESH)
     pl.semaphore_signal(barrier, inc=1, device_id={"seg": prev_seg}, device_id_type=MESH)
 
-    def to_features(ref, a):
+    def to_features(a):
+        loads[a].wait()
         for t in range(tiles):
-            send[a, t * 128 : (t + 1) * 128, :] = transposed(ref[:, t * 128 : (t + 1) * 128])
+            cols = slice(t * 128, (t + 1) * 128)
+            send[a, cols, :] = transposed(held_in[a, :, cols])
         recv[a, me] = send[a, head_rows(me), :]
 
     def in_copy(a, d, slot, sem_at):
@@ -89,21 +99,36 @@
             device_id_type=MESH,
         )
 
-    def send_in(a):
-        def body(i, carry):
-            d = lax.rem(me + i, n_dev)
-            in_copy(a, d, me, me).start()
-            return carry
-
-        lax.fori_loop(1, n_dev, body, 0)
-
-    to_features(k_ref, 1)
-    to_features(v_ref, 2)
+    def keys_in(d, slot, sem_at):
+        return pltpu.make_async_remote_copy(
+            src_ref=send.at[pl.ds(1, 2), head_rows(d)],
+            dst_ref=recv.at[pl.ds(1, 2), slot],
+            send_sem=in_ssem.at[1, d],
+            recv_sem=in_rsem.at[1, sem_at],
+            device_id={"dev": d},
+            device_id_type=MESH,
+        )
+
+    def nth_peer(i):
+        return lax.rem(me + 5 * i, n_dev)
+
+    def send_keys(i, carry):
+        keys_in(nth_peer(i), me, me).start()
+        return carry
+
+    to_features(1)
+    to_features(2)
     pl.semaphore_wait(barrier, n_dev + 1)
-    send_in(1)
-    send_in(2)
-    to_features(q_ref, 0)
-    send_in(0)
+    lax.fori_loop(1, n_dev, send_keys, 0)
+    to_features(0)
+
+    def send_queries(i, carry):
+        d = nth_peer(i)
+        keys_in(d, me, me).wait_send()
+        in_copy(0, d, me, me).start()
+        return carry
+
+    lax.fori_loop(1, n_dev, send_queries, 0)
 
     acc[...] = jnp.zeros_like(acc)
 
@@ -113,12 +138,12 @@
 
     def gather(i, carry):
         src = lax.rem(me - i + n_dev, n_dev)
+
+        @pl.when(i > 0)
+        def _():
+            keys_in(src, src, src).wait_recv()
+
         for a in (1, 2):
-
-            @pl.when(i > 0)
-            def _():
-                in_copy(a, src, src, src).wait_recv()
-
             place(a, src + far_blocks, recv[a, src])
         return carry
 
@@ -136,10 +161,6 @@
 
     for a in (1, 2):
         halo_copy(a).start()
-    for a in (1, 2):
-        halo_copy(a).wait_recv()
-        for b in range(far_blocks):
-            place(a, b, halo[a - 1, b])
 
     def out_copy(a, d, sem_at, head):
         return pltpu.make_async_remote_copy(
@@ -161,9 +182,27 @@
             out_send[a, block] = value
             out_copy(a, block, me, me).start()
 
+    def keys_out(d, sem_at, head):
+        return pltpu.make_async_remote_copy(
+            src_ref=out_send.at[pl.ds(1, 2), d],
+            dst_ref=out_recv.at[pl.ds(1, 2), head_rows(head)],
+            send_sem=out_ssem.at[1, d],
+            recv_sem=out_rsem.at[1, sem_at],
+            device_id={"dev": d},
+            device_id_type=MESH,
+        )
+
     def give_keys(block):
-        for a in (1, 2):
-            give(a, block, acc[a - 1, block + far_blocks].astype(BF16))
+        @pl.when(block == me)
+        def _():
+            for a in (1, 2):
+                out_recv[a, head_rows(me), :] = acc[a - 1, block + far_blocks].astype(BF16)
+
+        @pl.when(block != me)
+        def _():
+            for a in (1, 2):
+                out_send[a, block] = acc[a - 1, block + far_blocks].astype(BF16)
+            keys_out(block, me, me).start()
 
     def far_copy():
         return pltpu.make_async_remote_copy(
@@ -185,6 +224,13 @@
         @pl.when(s > 0)
         def _():
             in_copy(0, block, block, block).wait_recv()
+
+        @pl.when(s == jnp.maximum(me - far_blocks + 1, 0))
+        def _():
+            for a in (1, 2):
+                halo_copy(a).wait_recv()
+                for b in range(far_blocks):
+                    place(a, b, halo[a - 1, b])
 
         q_feat = recv[0, block]
         scores = jnp.dot(
@@ -255,7 +301,10 @@
 
                 @pl.when(head != me)
                 def _():
-                    out_copy(a, head, head, head).wait_recv()
+                    if a == 0:
+                        out_copy(a, head, head, head).wait_recv()
+                    elif a == 1:
+                        keys_out(head, head, head).wait_recv()
 
             for t in range(3 * g, 3 * g + 3):
                 cols = slice(t * 128, (t + 1) * 128)
@@ -263,9 +312,9 @@
 
     def drain(i, carry):
         d = lax.rem(me + i, n_dev)
-        for a in range(3):
-            in_copy(a, d, me, me).wait_send()
-            out_copy(a, d, me, me).wait_send()
+        in_copy(0, d, me, me).wait_send()
+        out_copy(0, d, me, me).wait_send()
+        keys_out(d, me, me).wait_send()
         return carry
 
     lax.fori_loop(1, n_dev, drain, 0)
@@ -284,9 +333,10 @@
     return pl.pallas_call(
         functools.partial(kernel, n_dev, n_seg),
         out_shape=[jax.ShapeDtypeStruct((frames, width), BF16)] * 3,
-        in_specs=[vmem] * 3,
+        in_specs=[pl.BlockSpec(memory_space=pltpu.HBM)] * 3,
         out_specs=[vmem] * 3,
         scratch_shapes=[
+            pltpu.VMEM((3, frames, width), BF16),
             pltpu.VMEM((3, width, frames), BF16),
             pltpu.VMEM((3, n_dev, dim, frames), BF16),
             pltpu.VMEM((2, far_blocks, dim, frames), BF16),
@@ -305,6 +355,7 @@
             dma,
             dma((3, n_dev)),
             dma((3, n_dev)),
+            dma((3,)),
         ],
         compiler_params=pltpu.CompilerParams(
             collective_id=0, has_side_effects=True, vmem_limit_bytes=48 << 20

time: 138 us -> 134 us (0.971)
  the two profiles are of different devices: /device:TPU:57 before, /device:TPU:64 now
where the time goes in v2:
time: 134 us
  Pallas kernels  128 us (96%)
  local copies, waits for them, and re-layouts  5.22 us (4%)
    pallas_call x1, Pallas kernels, local(): pl.pallas_call(functools.partial(kernel, n_dev, n_seg), out_shape=[jax.Sh...  128 us
    unnamed x9, local copies, waits for them, and re-layouts  5.22 us

profile of v2, /device:TPU:64, one launch (start us, length us, event | category | flops | bytes accessed | tf_op | source)
XLA Modules:
  0.0 133.7 jit_solution(11093636192160170233)
XLA Ops:
  0.6 0.0 copy-start
  0.6 1.0 copy-done
  1.6 0.0 copy-start.1
  1.6 1.0 copy-done.1
  2.6 0.0 copy-start.2
  2.6 1.0 copy-done.2
  3.6 127.8 %heads_exchange.1 = (bf16[128,1536]{1,0:T(8,128)(2,1)S(1)}, bf16[128,1536]{1,0:T(8,128)(2,1)S(1)}, bf16[128,1536]{1,0:T(8,128)(2,1)S(1)}) custom-call(bf16[128,1536]{1,0:T(8,128)(2,1)S(1)} %copy-done, bf16[128,1536]{1,0:T(8,128)(2,1)S(1)} %copy-done.1, bf16[128,1536]{1,0:T(8,128)(2,1)S(1)} %copy-done.2), custom_call_target="tpu_custom_call" | custom-call | tf_op jit(solution)/shard_map/heads_exchange/pallas_call | solution.py:333
  131.4 0.7 copy.9
  132.2 0.7 copy.10
  132.9 0.7 copy.11
Async XLA Ops:
  0.6 1.0 copy-start
  1.6 1.0 copy-start.1
  2.6 1.0 copy-start.2

commit v3 on v2

--- a/solution.py
+++ b/solution.py
@@ -26,9 +26,7 @@
     q_ref,
     k_ref,
     v_ref,
-    gq_ref,
-    gk_ref,
-    gv_ref,
+    out_recv,
     held_in,
     send,
     recv,
@@ -39,7 +37,6 @@
     far_out,
     far_in,
     out_send,
-    out_recv,
     in_ssem,
     in_rsem,
     halo_ssem,
@@ -49,6 +46,7 @@
     out_ssem,
     out_rsem,
     load_sem,
+    own_sem,
 ):
     me = lax.axis_index("dev")
     seg = lax.axis_index("seg")
@@ -172,14 +170,20 @@
             device_id_type=MESH,
         )
 
+    def own_copy(a):
+        return pltpu.make_async_copy(
+            out_send.at[a, me], out_recv.at[a, head_rows(me)], own_sem.at[a]
+        )
+
     def give(a, block, value):
+        out_send[a, block] = value
+
         @pl.when(block == me)
         def _():
-            out_recv[a, head_rows(me), :] = value
+            own_copy(a).start()
 
         @pl.when(block != me)
         def _():
-            out_send[a, block] = value
             out_copy(a, block, me, me).start()
 
     def keys_out(d, sem_at, head):
@@ -193,15 +197,16 @@
         )
 
     def give_keys(block):
+        for a in (1, 2):
+            out_send[a, block] = acc[a - 1, block + far_blocks].astype(BF16)
+
         @pl.when(block == me)
         def _():
             for a in (1, 2):
-                out_recv[a, head_rows(me), :] = acc[a - 1, block + far_blocks].astype(BF16)
+                own_copy(a).start()
 
         @pl.when(block != me)
         def _():
-            for a in (1, 2):
-                out_send[a, block] = acc[a - 1, block + far_blocks].astype(BF16)
             keys_out(block, me, me).start()
 
     def far_copy():
@@ -293,34 +298,39 @@
             acc[a, n_dev + b] += far_in[a, b].astype(F32)
         give_keys(n_dev - far_blocks + b)
 
-    group = 384 // dim
-    for a, out in ((0, gq_ref), (1, gk_ref), (2, gv_ref)):
-        for g in range(n_dev // group):
-            for i in range(group):
-                head = g * group + i
-
-                @pl.when(head != me)
-                def _():
-                    if a == 0:
-                        out_copy(a, head, head, head).wait_recv()
-                    elif a == 1:
-                        keys_out(head, head, head).wait_recv()
-
-            for t in range(3 * g, 3 * g + 3):
-                cols = slice(t * 128, (t + 1) * 128)
-                out[:, cols] = transposed(out_recv[a, cols, :])
-
     def drain(i, carry):
         d = lax.rem(me + i, n_dev)
         in_copy(0, d, me, me).wait_send()
         out_copy(0, d, me, me).wait_send()
         keys_out(d, me, me).wait_send()
+        out_copy(0, d, d, d).wait_recv()
+        keys_out(d, d, d).wait_recv()
         return carry
 
     lax.fori_loop(1, n_dev, drain, 0)
     for a in (1, 2):
         halo_copy(a).wait_send()
     far_copy().wait_send()
+    for a in range(3):
+        own_copy(a).wait()
+
+
+def to_frames(feat_ref, gq_ref, gk_ref, gv_ref, feat, held, load_sem, store_sem):
+    outs = (gq_ref, gk_ref, gv_ref)
+    loads = [
+        pltpu.make_async_copy(feat_ref.at[a], feat.at[a], load_sem.at[a]) for a in range(3)
+    ]
+    stores = [pltpu.make_async_copy(held.at[a], outs[a], store_sem.at[a]) for a in range(3)]
+    for load in loads:
+        load.start()
+    for a in range(3):
+        loads[a].wait()
+        for t in range(feat.shape[1] // 128):
+            cols = slice(t * 128, (t + 1) * 128)
+            held[a, :, cols] = transposed(feat[a, cols, :])
+        stores[a].start()
+    for store in stores:
+        store.wait()
 
 
 def local(n_dev, n_seg, queries, keys, values):
@@ -328,13 +338,13 @@
     dim = width // n_dev
     far_blocks = WINDOW // frames
     held = n_dev + far_blocks
-    vmem = pl.BlockSpec(memory_space=pltpu.VMEM)
     dma = pltpu.SemaphoreType.DMA
-    return pl.pallas_call(
+    hbm = pl.BlockSpec(memory_space=pltpu.HBM)
+    grads = pl.pallas_call(
         functools.partial(kernel, n_dev, n_seg),
-        out_shape=[jax.ShapeDtypeStruct((frames, width), BF16)] * 3,
-        in_specs=[pl.BlockSpec(memory_space=pltpu.HBM)] * 3,
-        out_specs=[vmem] * 3,
+        out_shape=jax.ShapeDtypeStruct((3, width, frames), BF16),
+        in_specs=[hbm] * 3,
+        out_specs=hbm,
         scratch_shapes=[
             pltpu.VMEM((3, frames, width), BF16),
             pltpu.VMEM((3, width, frames), BF16),
@@ -346,7 +356,6 @@
             pltpu.VMEM((2, far_blocks, dim, frames), BF16),
             pltpu.VMEM((2, far_blocks, dim, frames), BF16),
             pltpu.VMEM((3, n_dev, dim, frames), BF16),
-            pltpu.VMEM((3, width, frames), BF16),
             dma((3, n_dev)),
             dma((3, n_dev)),
             dma((2,)),
@@ -356,12 +365,27 @@
             dma((3, n_dev)),
             dma((3, n_dev)),
             dma((3,)),
+            dma((3,)),
         ],
         compiler_params=pltpu.CompilerParams(
-            collective_id=0, has_side_effects=True, vmem_limit_bytes=48 << 20
+            collective_id=0, has_side_effects=True, vmem_limit_bytes=60 << 20
         ),
         name="heads_exchange",
     )(queries, keys, values)
+    return pl.pallas_call(
+        to_frames,
+        out_shape=[jax.ShapeDtypeStruct((frames, width), BF16)] * 3,
+        in_specs=[hbm],
+        out_specs=[hbm] * 3,
+        scratch_shapes=[
+            pltpu.VMEM((3, width, frames), BF16),
+            pltpu.VMEM((3, frames, width), BF16),
+            dma((3,)),
+            dma((3,)),
+        ],
+        compiler_params=pltpu.CompilerParams(vmem_limit_bytes=60 << 20),
+        name="to_frames",
+    )(grads)
 
 
 def solution(mesh):

time: 134 us -> 130 us (0.970)
  the two profiles are of different devices: /device:TPU:64 before, /device:TPU:121 now
where the time goes in v3:
time: 130 us
  Pallas kernels  129 us (99%)
    pallas_call x1, Pallas kernels, local(): pl.pallas_call(functools.partial(kernel, n_dev, n_seg), out_shape=jax.Sha...  127 us

profile of v3, /device:TPU:121, one launch (start us, length us, event | category | flops | bytes accessed | tf_op | source)
XLA Modules:
  0.0 130.0 jit_solution(9751434225249170432)
XLA Ops:
  0.6 127.1 %heads_exchange.1.feat_ref = bf16[3,1536,128]{2,1,0:T(8,128)(2,1)} custom-call(bf16[128,1536]{1,0:T(8,128)(2,1)} %q_ref.1, bf16[128,1536]{1,0:T(8,128)(2,1)} %k_ref.1, bf16[128,1536]{1,0:T(8,128)(2,1)} %v_ref.1), custom_call_target="tpu_custom_call" | custom-call | tf_op jit(solution)/shard_map/heads_exchange/pallas_call | solution.py:343
  127.7 2.3 %to_frames.1 = (bf16[128,1536]{1,0:T(8,128)(2,1)}, bf16[128,1536]{1,0:T(8,128)(2,1)}, bf16[128,1536]{1,0:T(8,128)(2,1)}) custom-call(bf16[3,1536,128]{2,1,0:T(8,128)(2,1)} %heads_exchange.1.feat_ref), custom_call_target="tpu_custom_call" | custom-call | tf_op jit(solution)/shard_map/to_frames/pallas_call | solution.py:375

commit v4 on v3

--- a/solution.py
+++ b/solution.py
@@ -97,32 +97,27 @@
             device_id_type=MESH,
         )
 
-    def keys_in(d, slot, sem_at):
-        return pltpu.make_async_remote_copy(
-            src_ref=send.at[pl.ds(1, 2), head_rows(d)],
-            dst_ref=recv.at[pl.ds(1, 2), slot],
-            send_sem=in_ssem.at[1, d],
-            recv_sem=in_rsem.at[1, sem_at],
-            device_id={"dev": d},
-            device_id_type=MESH,
-        )
-
     def nth_peer(i):
         return lax.rem(me + 5 * i, n_dev)
 
-    def send_keys(i, carry):
-        keys_in(nth_peer(i), me, me).start()
-        return carry
+    def send_in(a):
+        def body(i, carry):
+            in_copy(a, nth_peer(i), me, me).start()
+            return carry
+
+        lax.fori_loop(1, n_dev, body, 0)
 
     to_features(1)
+    pl.semaphore_wait(barrier, n_dev + 1)
+    send_in(1)
     to_features(2)
-    pl.semaphore_wait(barrier, n_dev + 1)
-    lax.fori_loop(1, n_dev, send_keys, 0)
+    send_in(2)
     to_features(0)
 
     def send_queries(i, carry):
         d = nth_peer(i)
-        keys_in(d, me, me).wait_send()
+        for a in (1, 2):
+            in_copy(a, d, me, me).wait_send()
         in_copy(0, d, me, me).start()
         return carry
 
@@ -139,7 +134,8 @@
 
         @pl.when(i > 0)
         def _():
-            keys_in(src, src, src).wait_recv()
+            for a in (1, 2):
+                in_copy(a, src, src, src).wait_recv()
 
         for a in (1, 2):
             place(a, src + far_blocks, recv[a, src])

time: 130 us -> 130 us (level)
  no operation moved by 1% of the time
where the time goes in v4:
time: 130 us
  Pallas kernels  130 us (100%)
    pallas_call x1, Pallas kernels, local(): pl.pallas_call(functools.partial(kernel, n_dev, n_seg), out_shape=jax.Sha...  127 us

profile of v4, /device:TPU:121, one launch (start us, length us, event | category | flops | bytes accessed | tf_op | source)
XLA Modules:
  0.0 130.3 jit_solution(7319884030305649028)
XLA Ops:
  0.6 127.4 %heads_exchange.1.feat_ref = bf16[3,1536,128]{2,1,0:T(8,128)(2,1)} custom-call(bf16[128,1536]{1,0:T(8,128)(2,1)} %q_ref.1, bf16[128,1536]{1,0:T(8,128)(2,1)} %k_ref.1, bf16[128,1536]{1,0:T(8,128)(2,1)} %v_ref.1), custom_call_target="tpu_custom_call" | custom-call | tf_op jit(solution)/shard_map/heads_exchange/pallas_call | solution.py:339
  128.0 2.3 %to_frames.1 = (bf16[128,1536]{1,0:T(8,128)(2,1)}, bf16[128,1536]{1,0:T(8,128)(2,1)}, bf16[128,1536]{1,0:T(8,128)(2,1)}) custom-call(bf16[3,1536,128]{2,1,0:T(8,128)(2,1)} %heads_exchange.1.feat_ref), custom_call_target="tpu_custom_call" | custom-call | tf_op jit(solution)/shard_map/to_frames/pallas_call | solution.py:371
